TPU v7x, 256 devices: a whole 4x4x8 slice. The times are simulated.
256 devices in a mesh: cube: 8 (over z), front: 32 (over x, y, core).
Axes of the slice: x: 4, y: 4, z: 8, core: 2. Of those that a mesh axis runs over, the one named last changes fastest.
Arguments:
- right_sides: float32 [3, 8, 2048, 128], P(None, 'cube', 'front'), may hold values from -6 to 6
- inverse_leaf: float32 [8, 2048, 2048], P('cube', 'front'), may hold values from -2 to 2, as said below
- inverse_mid: float32 [8, 2048, 4096], P('cube', 'front'), may hold values from -2 to 2, as said below
- inverse_top: float32 [8, 2048, 8192], P('cube', 'front'), may hold values from -2 to 2, as said below
- coupling_mid: float32 [8, 2048, 4096], P('cube', 'front'), may hold values from -0.1875 to 0.1875
- coupling_top: float32 [8, 2048, 8192], P('cube', 'front'), may hold values from -0.125 to 0.125
- pattern_mid: int32 [8, 32, 64], P('cube', 'front'), may hold values 0 or 1
- pattern_top: int32 [8, 32, 128], P('cube', 'front'), may hold values 0 or 1
Outputs:
- solution: float32 [3, 8, 2048, 128], P(None, 'cube', 'front')
Inputs may be any that keep to these rules, and one draw needn't show every extreme that they name: `inverse_leaf`: each block is the inverse of a lower triangular diagonal block: zero above the diagonal of the separator's row order, diagonal 1 to 2. `inverse_mid`: as inverse_leaf. `inverse_top`: as inverse_leaf.
All inputs are finite; a program needn't handle non-finite values. No bound on the sum of `pattern_mid` or of `pattern_top` on one device may be relied on, other than what follows from the above.
Results may differ from a plain program's by a relative error of at most 0.00013.
Values sent between devices are 32-bit elements; how exact they have to be, the bound alone decides.
A program may use at most 64 MiB of HBM per device.

v0:
```python
import jax
import jax.numpy as jnp
from jax import lax
from jax.sharding import PartitionSpec as P

TILE = 64


def from_behind(array, axis, by):
    devices = lax.axis_size(axis)
    pairs = [(i, i + by) for i in range(devices) if 0 <= i + by < devices]
    return lax.ppermute(array, axis, pairs)


def masked(coupling, pattern):
    keep_rows = jnp.repeat(pattern[0], TILE, axis=0)
    keep_all = jnp.repeat(keep_rows, TILE, axis=1)
    return coupling[0] * keep_all.astype(jnp.float32)


def members_of(local_rows, count, cube_pos):
    if count == 1:
        return local_rows[None]
    copies = []
    for distance in range(-(count - 1), count):
        if distance == 0:
            copies.append(local_rows)
        else:
            copies.append(from_behind(local_rows, "cube", distance))
    every_copy = jnp.stack(copies, 0)
    member_pos = cube_pos % count
    wanted = member_pos - jnp.arange(count, dtype=jnp.int32) + (count - 1)
    return jnp.take(every_copy, wanted, axis=0)


def gathered_product(matrix, stacked):
    count = stacked.shape[0]
    height = matrix.shape[0]
    member_width = matrix.shape[1] // count
    shaped = matrix.reshape(height, count, member_width)
    return jnp.einsum(
        "rms,msn->rn",
        shaped,
        lax.all_gather(stacked, "front", axis=1, tiled=True),
        precision=lax.Precision.HIGHEST,
        preferred_element_type=jnp.float32,
    )


def spread_back(matrix, local_rows, count, cube_pos):
    height = matrix.shape[0]
    member_width = matrix.shape[1] // count
    shaped = matrix.reshape(height, count, member_width)
    summed = lax.psum_scatter(
        jnp.einsum(
            "rms,rn->smn",
            shaped,
            local_rows,
            precision=lax.Precision.HIGHEST,
            preferred_element_type=jnp.float32,
        ),
        "front",
        scatter_dimension=0,
        tiled=True,
    )
    if count == 1:
        return summed[:, 0]
    start_pos = cube_pos // count * count
    zeros_all = jnp.zeros((height, lax.axis_size("cube"), summed.shape[2]), jnp.float32)
    placed = lax.dynamic_update_slice_in_dim(zeros_all, summed, start_pos, 1)
    return lax.psum_scatter(placed, "cube", scatter_dimension=1, tiled=True)[:, 0]


def local(
    right_sides,
    inverse_leaf,
    inverse_mid,
    inverse_top,
    coupling_mid,
    coupling_top,
    pattern_mid,
    pattern_top,
):
    cube_pos = lax.axis_index("cube")
    block_mid = masked(coupling_mid, pattern_mid)
    block_top = masked(coupling_top, pattern_top)
    inv_leaf = inverse_leaf[0]
    inv_mid = inverse_mid[0]
    inv_top = inverse_top[0]
    sides = right_sides[:, 0]
    solved_leaf = gathered_product(inv_leaf, members_of(sides[0], 1, cube_pos))
    update_mid = gathered_product(block_mid, members_of(solved_leaf, 2, cube_pos))
    solved_mid = gathered_product(inv_mid, members_of(sides[1] - update_mid, 2, cube_pos))
    update_top = gathered_product(block_top, members_of(solved_mid, 4, cube_pos))
    solved_top = gathered_product(inv_top, members_of(sides[2] - update_top, 4, cube_pos))
    back_top = spread_back(inv_top, solved_top, 4, cube_pos)
    carry_mid = spread_back(block_top, back_top, 4, cube_pos)
    back_mid = spread_back(inv_mid, solved_mid - carry_mid, 2, cube_pos)
    carry_leaf = spread_back(block_mid, back_mid, 2, cube_pos)
    back_leaf = spread_back(inv_leaf, solved_leaf - carry_leaf, 1, cube_pos)
    result = jnp.stack([back_leaf, back_mid, back_top])
    return result[:, None]


def solution(mesh):
    return jax.shard_map(
        local,
        mesh=mesh,
        in_specs=(
            P(None, "cube", "front", None),
            P("cube", "front", None),
            P("cube", "front", None),
            P("cube", "front", None),
            P("cube", "front", None),
            P("cube", "front", None),
            P("cube", "front", None),
            P("cube", "front", None),
        ),
        out_specs=P(None, "cube", "front", None),
        check_vma=False,
    )
```

profile of v0, /device:TPU:2, one launch (start us, length us, event | category | flops | bytes accessed | tf_op | source)
XLA Modules:
  0.0 978.9 jit_solution(17281980897856328411)
XLA Ops:
  8.2 52.2 %all-gather.15.cloned.1.call-done = f32[1,1,2048,128]{3,2,1,0:T(8,128)} async-done(((f32[1,1,64,128]{3,2,1,0:T(8,128)}), f32[1,1,2048,128]{3,2,1,0:T(8,128)}) %all-gather.15.cloned.1.call-update) | async-done | bytes 1048592 | tf_op jit(solution)/shard_map/all_gather | solution.py:44
  63.6 4.5 collective-permute-start.1
  72.3 49.0 %all-gather.7.cloned.1.call-done = f32[2,2048,128]{2,1,0:T(8,128)} async-done(((f32[2,64,128]{2,1,0:T(8,128)}), f32[2,2048,128]{2,1,0:T(8,128)}) %all-gather.7.cloned.1.call-update) | async-done | bytes 2097168 | tf_op jit(solution)/shard_map/all_gather | solution.py:44
  121.3 3.5 fusion.6
  126.2 4.5 collective-permute-start.3
  134.6 49.3 %all-gather.9.cloned.1.call-done = f32[2,2048,128]{2,1,0:T(8,128)} async-done(((f32[2,64,128]{2,1,0:T(8,128)}), f32[2,2048,128]{2,1,0:T(8,128)}) %all-gather.9.cloned.1.call-update) | async-done | bytes 2097168 | tf_op jit(solution)/shard_map/all_gather | solution.py:44
  183.9 3.5 fusion.13
  191.3 4.5 collective-permute-start.7
  195.9 5.5 collective-permute-start.8
  201.4 7.5 collective-permute-start.9
  212.2 2.7 squeeze.30
  215.2 48.2 %all-gather.11.cloned.1.call-done = f32[4,2048,128]{2,1,0:T(8,128)} async-done(((f32[4,64,128]{2,1,0:T(8,128)}), f32[4,2048,128]{2,1,0:T(8,128)}) %all-gather.11.cloned.1.call-update) | async-done | bytes 4194320 | tf_op jit(solution)/shard_map/all_gather | solution.py:44
  263.3 5.9 fusion.7
  273.1 4.5 collective-permute-start.13
  277.7 5.5 collective-permute-start.14
  283.2 7.5 collective-permute-start.15
  296.9 48.3 %all-gather.13.cloned.1.call-done = f32[4,2048,128]{2,1,0:T(8,128)} async-done(((f32[4,64,128]{2,1,0:T(8,128)}), f32[4,2048,128]{2,1,0:T(8,128)}) %all-gather.13.cloned.1.call-update) | async-done | bytes 4194320 | tf_op jit(solution)/shard_map/all_gather | solution.py:44
  345.2 5.9 fusion.2
  351.1 8.4 convolution_bitcast_fusion.1
  359.8 88.9 %reduce-scatter.10.cloned.1.call-done = f32[64,4,128]{2,0,1:T(8,128)} async-done(((f32[2048,4,128]{2,0,1:T(8,128)}), f32[64,4,128]{2,0,1:T(8,128)}) %reduce-scatter.10.cloned.1.call-update) | async-done | bytes 131088 | tf_op jit(solution)/shard_map/reduce_scatter | solution.py:54
  454.8 33.0 %reduce-scatter.12.cloned.1.call-done = f32[64,1,128]{2,0,1:T(8,128)} async-done(((f32[64,8,128]{2,0,1:T(8,128)}), f32[64,1,128]{2,0,1:T(8,128)}) %reduce-scatter.12.cloned.1.call-update) | async-done | bytes 32784 | tf_op jit(solution)/shard_map/reduce_scatter | solution.py:71
  487.8 9.2 convolution_bitcast_fusion
  497.1 87.9 %reduce-scatter.14.cloned.1.call-done = f32[64,4,128]{2,0,1:T(8,128)} async-done(((f32[2048,4,128]{2,0,1:T(8,128)}), f32[64,4,128]{2,0,1:T(8,128)}) %reduce-scatter.14.cloned.1.call-update) | async-done | bytes 131088 | tf_op jit(solution)/shard_map/reduce_scatter | solution.py:54
  586.7 37.4 %reduce-scatter.16.cloned.1.call-done = f32[64,1,128]{2,0,1:T(8,128)} async-done(((f32[64,8,128]{2,0,1:T(8,128)}), f32[64,1,128]{2,0,1:T(8,128)}) %reduce-scatter.16.cloned.1.call-update) | async-done | bytes 32784 | tf_op jit(solution)/shard_map/reduce_scatter | solution.py:71
  624.1 5.7 convolution_bitcast_fusion.3
  630.1 84.6 %reduce-scatter.18.cloned.1.call-done = f32[64,2,128]{2,0,1:T(8,128)} async-done(((f32[2048,2,128]{2,0,1:T(8,128)}), f32[64,2,128]{2,0,1:T(8,128)}) %reduce-scatter.18.cloned.1.call-update) | async-done | bytes 65552 | tf_op jit(solution)/shard_map/reduce_scatter | solution.py:54
  717.6 36.1 %reduce-scatter.20.cloned.1.call-done = f32[64,1,128]{2,0,1:T(8,128)} async-done(((f32[64,8,128]{2,0,1:T(8,128)}), f32[64,1,128]{2,0,1:T(8,128)}) %reduce-scatter.20.cloned.1.call-update) | async-done | bytes 32784 | tf_op jit(solution)/shard_map/reduce_scatter | solution.py:71
  753.7 5.7 convolution_bitcast_fusion.2
  759.5 84.9 %reduce-scatter.22.cloned.1.call-done = f32[64,2,128]{2,0,1:T(8,128)} async-done(((f32[2048,2,128]{2,0,1:T(8,128)}), f32[64,2,128]{2,0,1:T(8,128)}) %reduce-scatter.22.cloned.1.call-update) | async-done | bytes 65552 | tf_op jit(solution)/shard_map/reduce_scatter | solution.py:54
  846.1 37.5 %reduce-scatter.24.cloned.1.call-done = f32[64,1,128]{2,0,1:T(8,128)} async-done(((f32[64,8,128]{2,0,1:T(8,128)}), f32[64,1,128]{2,0,1:T(8,128)}) %reduce-scatter.24.cloned.1.call-update) | async-done | bytes 32784 | tf_op jit(solution)/shard_map/reduce_scatter | solution.py:71
  883.6 3.6 convolution_bitcast_fusion.4
  887.2 83.6 %reduce-scatter.26.cloned.1.call-done = f32[64,1,128]{2,0,1:T(8,128)} async-done(((f32[2048,1,128]{2,0,1:T(8,128)}), f32[64,1,128]{2,0,1:T(8,128)}) %reduce-scatter.26.cloned.1.call-update) | async-done | bytes 32784 | tf_op jit(solution)/shard_map/reduce_scatter | solution.py:54
  (146 shorter events, 45.4 us)
Async XLA Ops:
  6.5 53.8 %all-gather.15.cloned.1.call-start = ((), (), s32[]{:S(2)}) async-start(), calls=%async_computation.22 | async-start | bytes 1081344 | tf_op jit(solution)/shard_map/all_gather | solution.py:44
  8.1 113.3 %all-gather.7.cloned.1.call-start = ((), (), s32[]{:S(2)}) async-start(), calls=%async_computation.9 | async-start | bytes 2162688 | tf_op jit(solution)/shard_map/all_gather | solution.py:44
  62.3 5.9 collective-permute-start
  63.6 6.1 collective-permute-start.1
  71.1 112.8 %all-gather.9.cloned.1.call-start = ((), (), s32[]{:S(2)}) async-start(), calls=%async_computation.10 | async-start | bytes 2162688 | tf_op jit(solution)/shard_map/all_gather | solution.py:44
  124.9 5.9 collective-permute-start.2
  126.2 6.1 collective-permute-start.3
  133.6 129.7 %all-gather.11.cloned.1.call-start = ((), (), s32[]{:S(2)}) async-start(), calls=%async_computation.11 | async-start | bytes 4325376 | tf_op jit(solution)/shard_map/all_gather | solution.py:44
  187.4 14.0 %collective-permute-start.4 = (f32[64,128]{1,0:T(8,128)S(1)}, f32[64,128]{1,0:T(8,128)S(1)}, u32[]{:S(2)}, u32[]{:S(2)}) collective-permute-start(f32[64,128]{1,0:T(8,128)S(1)} %bitcast.110), channel_id=1, source_target_pairs={{96,0},{128,32},{160,64},{192,96},{224,128},{97,1},{129,33},{161,6... | collective-permute-start | bytes 98312 | tf_op jit(solution)/shard_map/ppermute | solution.py:12
  188.7 20.2 %collective-permute-start.5 = (f32[64,128]{1,0:T(8,128)S(1)}, f32[64,128]{1,0:T(8,128)S(1)}, u32[]{:S(2)}, u32[]{:S(2)}) collective-permute-start(f32[64,128]{1,0:T(8,128)S(1)} %bitcast.111), channel_id=1, source_target_pairs={{64,0},{96,32},{128,64},{160,96},{192,128},{224,160},{65,1},{97,33... | collective-permute-start | bytes 98312 | tf_op jit(solution)/shard_map/ppermute | solution.py:12
  190.0 18.9 %collective-permute-start.6 = (f32[64,128]{1,0:T(8,128)S(1)}, f32[64,128]{1,0:T(8,128)S(1)}, u32[]{:S(2)}, u32[]{:S(2)}) collective-permute-start(f32[64,128]{1,0:T(8,128)S(1)} %bitcast.112), channel_id=1, source_target_pairs={{32,0},{64,32},{96,64},{128,96},{160,128},{192,160},{224,192},{33,... | collective-permute-start | bytes 98312 | tf_op jit(solution)/shard_map/ppermute | solution.py:12
  191.3 17.7 %collective-permute-start.7 = (f32[64,128]{1,0:T(8,128)S(1)}, f32[64,128]{1,0:T(8,128)S(1)}, u32[]{:S(2)}, u32[]{:S(2)}) collective-permute-start(f32[64,128]{1,0:T(8,128)S(1)} %bitcast.113), channel_id=1, source_target_pairs={{0,32},{32,64},{64,96},{96,128},{128,160},{160,192},{192,224},{1,3... | collective-permute-start | bytes 98312 | tf_op jit(solution)/shard_map/ppermute | solution.py:12
  195.9 13.1 %collective-permute-start.8 = (f32[64,128]{1,0:T(8,128)S(1)}, f32[64,128]{1,0:T(8,128)S(1)}, u32[]{:S(2)}, u32[]{:S(2)}) collective-permute-start(f32[64,128]{1,0:T(8,128)S(1)} %bitcast.114), channel_id=1, source_target_pairs={{0,64},{32,96},{64,128},{96,160},{128,192},{160,224},{1,65},{33,97... | collective-permute-start | bytes 98312 | tf_op jit(solution)/shard_map/ppermute | solution.py:12
  201.4 9.1 collective-permute-start.9
  211.8 133.3 %all-gather.13.cloned.1.call-start = ((), (), s32[]{:S(2)}) async-start(), calls=%async_computation.12 | async-start | bytes 4325376 | tf_op jit(solution)/shard_map/all_gather | solution.py:44
  269.2 14.0 %collective-permute-start.10 = (f32[64,128]{1,0:T(8,128)S(1)}, f32[64,128]{1,0:T(8,128)S(1)}, u32[]{:S(2)}, u32[]{:S(2)}) collective-permute-start(f32[64,128]{1,0:T(8,128)S(1)} %fusion.7), channel_id=1, source_target_pairs={{96,0},{128,32},{160,64},{192,96},{224,128},{97,1},{129,33},{161,6... | collective-permute-start | bytes 98312 | tf_op jit(solution)/shard_map/ppermute | solution.py:12
  270.5 20.2 %collective-permute-start.11 = (f32[64,128]{1,0:T(8,128)S(1)}, f32[64,128]{1,0:T(8,128)S(1)}, u32[]{:S(2)}, u32[]{:S(2)}) collective-permute-start(f32[64,128]{1,0:T(8,128)S(1)} %fusion.7), channel_id=1, source_target_pairs={{64,0},{96,32},{128,64},{160,96},{192,128},{224,160},{65,1},{97,33... | collective-permute-start | bytes 98312 | tf_op jit(solution)/shard_map/ppermute | solution.py:12
  271.8 18.9 %collective-permute-start.12 = (f32[64,128]{1,0:T(8,128)S(1)}, f32[64,128]{1,0:T(8,128)S(1)}, u32[]{:S(2)}, u32[]{:S(2)}) collective-permute-start(f32[64,128]{1,0:T(8,128)S(1)} %fusion.7), channel_id=1, source_target_pairs={{32,0},{64,32},{96,64},{128,96},{160,128},{192,160},{224,192},{33,... | collective-permute-start | bytes 98312 | tf_op jit(solution)/shard_map/ppermute | solution.py:12
  273.1 17.7 %collective-permute-start.13 = (f32[64,128]{1,0:T(8,128)S(1)}, f32[64,128]{1,0:T(8,128)S(1)}, u32[]{:S(2)}, u32[]{:S(2)}) collective-permute-start(f32[64,128]{1,0:T(8,128)S(1)} %fusion.7), channel_id=1, source_target_pairs={{0,32},{32,64},{64,96},{96,128},{128,160},{160,192},{192,224},{1,3... | collective-permute-start | bytes 98312 | tf_op jit(solution)/shard_map/ppermute | solution.py:12
  277.7 13.1 %collective-permute-start.14 = (f32[64,128]{1,0:T(8,128)S(1)}, f32[64,128]{1,0:T(8,128)S(1)}, u32[]{:S(2)}, u32[]{:S(2)}) collective-permute-start(f32[64,128]{1,0:T(8,128)S(1)} %fusion.7), channel_id=1, source_target_pairs={{0,64},{32,96},{64,128},{96,160},{128,192},{160,224},{1,65},{33,97... | collective-permute-start | bytes 98312 | tf_op jit(solution)/shard_map/ppermute | solution.py:12
  283.2 9.1 collective-permute-start.15
  293.6 155.0 %reduce-scatter.10.cloned.1.call-start = ((), (), s32[]{:S(2)}) async-start(), calls=%async_computation.13 | async-start | bytes 4325376 | tf_op jit(solution)/shard_map/reduce_scatter | solution.py:54
  359.5 128.2 %reduce-scatter.12.cloned.1.call-start = ((), (), s32[]{:S(2)}) async-start(), calls=%async_computation.14 | async-start | bytes 294912 | tf_op jit(solution)/shard_map/reduce_scatter | solution.py:71
  450.3 134.6 %reduce-scatter.14.cloned.1.call-start = ((), (), s32[]{:S(2)}) async-start(), calls=%async_computation.15 | async-start | bytes 4325376 | tf_op jit(solution)/shard_map/reduce_scatter | solution.py:54
  497.0 127.1 %reduce-scatter.16.cloned.1.call-start = ((), (), s32[]{:S(2)}) async-start(), calls=%async_computation.16 | async-start | bytes 294912 | tf_op jit(solution)/shard_map/reduce_scatter | solution.py:71
  586.6 128.1 %reduce-scatter.18.cloned.1.call-start = ((), (), s32[]{:S(2)}) async-start(), calls=%async_computation.17 | async-start | bytes 2162688 | tf_op jit(solution)/shard_map/reduce_scatter | solution.py:54
  629.9 123.9 %reduce-scatter.20.cloned.1.call-start = ((), (), s32[]{:S(2)}) async-start(), calls=%async_computation.18 | async-start | bytes 294912 | tf_op jit(solution)/shard_map/reduce_scatter | solution.py:71
  716.3 128.2 %reduce-scatter.22.cloned.1.call-start = ((), (), s32[]{:S(2)}) async-start(), calls=%async_computation.19 | async-start | bytes 2162688 | tf_op jit(solution)/shard_map/reduce_scatter | solution.py:54
  759.5 211.3 %copy-start.11 = (f32[64,1,128]{2,0,1:T(8,128)S(1)}, f32[64,1,128]{2,0,1:T(8,128)}, u32[]{:S(2)}) copy-start(f32[64,1,128]{2,0,1:T(8,128)} %reduce-scatter.12.cloned.1.call-done) | copy-start | bytes 98308
  759.5 211.3 %copy-start.12 = (f32[64,1,128]{2,0,1:T(8,128)S(1)}, f32[64,1,128]{2,0,1:T(8,128)}, u32[]{:S(2)}) copy-start(f32[64,1,128]{2,0,1:T(8,128)} %reduce-scatter.20.cloned.1.call-done) | copy-start | bytes 98308
  759.5 124.1 %reduce-scatter.24.cloned.1.call-start = ((), (), s32[]{:S(2)}) async-start(), calls=%async_computation.20 | async-start | bytes 294912 | tf_op jit(solution)/shard_map/reduce_scatter | solution.py:71
  846.1 124.7 %reduce-scatter.26.cloned.1.call-start = ((), (), s32[]{:S(2)}) async-start(), calls=%async_computation.21 | async-start | bytes 1081344 | tf_op jit(solution)/shard_map/reduce_scatter | solution.py:54
  (14 other events, 745.1 us)
Sparse Core Ops, SparseCore 0:
  9.9 50.4 all-gather.14
  71.2 50.1 all-gather.6
  133.7 50.1 all-gather.8
  211.9 51.3 all-gather.10
  293.8 51.3 all-gather.12
  359.7 88.9 reduce-scatter.9
  451.3 36.4 reduce-scatter.11
  497.1 87.7 reduce-scatter.13
  587.6 36.4 reduce-scatter.15
  630.0 84.7 reduce-scatter.17
  717.2 36.4 reduce-scatter.19
  759.6 84.8 reduce-scatter.21
  847.1 36.4 reduce-scatter.23
  887.3 83.4 reduce-scatter.25
where the time goes:
time: 986 us; the launch traced here: 979 us
  waiting for transfers between devices  827 us (84%)
  starting transfers between devices  56.3 us (6%)
  matrix products  53.5 us (5%)
  local copies, waits for them, and re-layouts  21.7 us (2%)
  between operations  14.2 us (1%)
    reduce_scatter x5, waiting for transfers between devices, spread_back(): lax.psum_scatter(jnp.einsum('rms,rn->smn', shaped, local_rows, precision=...  430 us
    all_gather x5, waiting for transfers between devices, gathered_product(): lax.all_gather(stacked, 'front', axis=1, tiled=True)  247 us
    reduce_scatter x4, waiting for transfers between devices, spread_back(): lax.psum_scatter(placed, 'cube', scatter_dimension=1, tiled=True)[:, 0]  144 us
    ppermute x16, starting transfers between devices, from_behind(): return lax.ppermute(array, axis, pairs)  54.5 us
    dot_general x5, matrix products, spread_back(): jnp.einsum('rms,rn->smn', shaped, local_rows, precision=lax.Precision.HIG...  32.6 us
    dot_general x5, matrix products, gathered_product(): jnp.einsum('rms,msn->rn', shaped, lax.all_gather(stacked, 'front', axis=1...  20.8 us
  transfers between devices with their start and end apart: 30, of which 18 were waited for; matrix products, arithmetic and copies ran while one was open for 1% of the time, Pallas kernels for 0%

commit v1 on v0

--- a/solution.py
+++ b/solution.py
@@ -41,7 +41,9 @@
     return jnp.einsum(
         "rms,msn->rn",
         shaped,
-        lax.all_gather(stacked, "front", axis=1, tiled=True),
+        jnp.concatenate(
+            lax.all_to_all(jnp.stack([stacked] * lax.axis_size("front")), "front", 0, 0), axis=1
+        ),
         precision=lax.Precision.HIGHEST,
         preferred_element_type=jnp.float32,
     )

time: 986 us -> 954 us (0.968)
  waiting for transfers between devices: 827 us -> 746 us
  starting transfers between devices: 56.3 us -> 99.9 us
  local copies, waits for them, and re-layouts: 21.7 us -> 36.1 us
    all_gather x5 -> x0, waiting for transfers between devices: 247 us -> none  [gathered_product(): lax.all_gather(stacked, 'front', axis=1, tiled=True)]
    all_to_all x0 -> x5, waiting for transfers between devices: none -> 156 us  [gathered_product(): lax.all_to_all(jnp.stack([stacked] * lax.axis_size('front')), 'front', 0, 0)]
    all_to_all x0 -> x5, starting transfers between devices: none -> 40.4 us  [gathered_product(): lax.all_to_all(jnp.stack([stacked] * lax.axis_size('front')), 'front', 0, 0)]
    another operation x4 -> x10, local copies, waits for them, and re-layouts: 0.07 us -> 10.3 us  [the longest x6 10.2 us: gathered_product(): jnp.stack([stacked] * lax.axis_size('front'))]
  transfers between devices with their start and end apart: 30 -> 30, of which waited for: 18 -> 20; matrix products, arithmetic and copies ran while one was open for 1% -> 1% of each run, Pallas kernels for 0% -> 0%
where the time goes in v1:
time: 954 us; the launch traced here: 944 us
  waiting for transfers between devices  746 us (78%)
  starting transfers between devices  99.9 us (10%)
  matrix products  44.7 us (5%)
  local copies, waits for them, and re-layouts  36.1 us (4%)
  between operations  14.2 us (1%)
    reduce_scatter x5, waiting for transfers between devices, spread_back(): lax.psum_scatter(jnp.einsum('rms,rn->smn', shaped, local_rows, precision=...  435 us
    all_to_all x5, waiting for transfers between devices, gathered_product(): lax.all_to_all(jnp.stack([stacked] * lax.axis_size('front')), 'front', 0, 0)  156 us
    reduce_scatter x4, waiting for transfers between devices, spread_back(): lax.psum_scatter(placed, 'cube', scatter_dimension=1, tiled=True)[:, 0]  149 us
    ppermute x16, starting transfers between devices, from_behind(): return lax.ppermute(array, axis, pairs)  58.7 us
    all_to_all x5, starting transfers between devices, gathered_product(): lax.all_to_all(jnp.stack([stacked] * lax.axis_size('front')), 'front', 0, 0)  40.4 us
    dot_general x5, matrix products, spread_back(): jnp.einsum('rms,rn->smn', shaped, local_rows, precision=lax.Precision.HIG...  32.6 us
  transfers between devices with their start and end apart: 30, of which 20 were waited for; matrix products, arithmetic and copies ran while one was open for 1% of the time, Pallas kernels for 0%

profile of v1, /device:TPU:2, one launch (start us, length us, event | category | flops | bytes accessed | tf_op | source)
XLA Modules:
  0.0 944.4 jit_solution(11613919764035640651)
XLA Ops:
  8.5 7.6 all-to-all-start
  16.1 14.4 %all-to-all-done = f32[32,1,64,128]{3,2,1,0:T(8,128)S(1)} async-done(((f32[32,1,64,128]{3,2,1,0:T(8,128)}), f32[32,1,64,128]{3,2,1,0:T(8,128)S(1)}, u32[]{:S(2)}, u32[]{:S(2)}) %all-to-all-start) | async-done | bytes 1048608 | tf_op jit(solution)/shard_map/all_to_all | solution.py:45
  32.6 4.5 collective-permute-start.1
  40.9 7.1 all-to-all-start.1
  49.2 24.8 %all-to-all-done.1 = f32[32,2,64,128]{3,2,1,0:T(8,128)} async-done(((f32[32,2,64,128]{3,2,1,0:T(8,128)}), f32[32,2,64,128]{3,2,1,0:T(8,128)}, u32[]{:S(2)}, u32[]{:S(2)}) %all-to-all-start.1) | async-done | bytes 2097184 | tf_op jit(solution)/shard_map/all_to_all | solution.py:45
  79.1 4.9 collective-permute-start.3
  87.8 7.8 all-to-all-start.2
  96.5 25.0 %all-to-all-done.2 = f32[32,2,64,128]{3,2,1,0:T(8,128)} async-done(((f32[32,2,64,128]{3,2,1,0:T(8,128)}), f32[32,2,64,128]{3,2,1,0:T(8,128)}, u32[]{:S(2)}, u32[]{:S(2)}) %all-to-all-start.2) | async-done | bytes 2097184 | tf_op jit(solution)/shard_map/all_to_all | solution.py:45
  129.2 4.9 collective-permute-start.7
  134.1 8.5 collective-permute-start.8
  142.6 7.8 collective-permute-start.9
  155.1 8.5 all-to-all-start.3
  168.0 45.5 %all-to-all-done.3 = f32[32,4,64,128]{3,2,1,0:T(8,128)} async-done(((f32[32,4,64,128]{3,2,1,0:T(8,128)}), f32[32,4,64,128]{3,2,1,0:T(8,128)}, u32[]{:S(2)}, u32[]{:S(2)}) %all-to-all-start.3) | async-done | bytes 4194336 | tf_op jit(solution)/shard_map/all_to_all | solution.py:45
  223.6 4.5 collective-permute-start.13
  228.2 5.8 collective-permute-start.14
  234.0 7.5 collective-permute-start.15
  246.3 9.4 all-to-all-start.4
  259.5 46.4 %all-to-all-done.4 = f32[32,4,64,128]{3,2,1,0:T(8,128)} async-done(((f32[32,4,64,128]{3,2,1,0:T(8,128)}), f32[32,4,64,128]{3,2,1,0:T(8,128)}, u32[]{:S(2)}, u32[]{:S(2)}) %all-to-all-start.4) | async-done | bytes 4194336 | tf_op jit(solution)/shard_map/all_to_all | solution.py:45
  308.8 3.7 fusion.1
  312.5 8.4 convolution_bitcast_fusion.1
  321.0 93.3 %reduce-scatter.10.cloned.1.call-done = f32[64,4,128]{2,0,1:T(8,128)} async-done(((f32[2048,4,128]{2,0,1:T(8,128)}), f32[64,4,128]{2,0,1:T(8,128)}) %reduce-scatter.10.cloned.1.call-update) | async-done | bytes 131088 | tf_op jit(solution)/shard_map/reduce_scatter | solution.py:56
  416.2 37.2 %reduce-scatter.12.cloned.1.call-done = f32[64,1,128]{2,0,1:T(8,128)} async-done(((f32[64,8,128]{2,0,1:T(8,128)}), f32[64,1,128]{2,0,1:T(8,128)}) %reduce-scatter.12.cloned.1.call-update) | async-done | bytes 32784 | tf_op jit(solution)/shard_map/reduce_scatter | solution.py:73
  453.4 9.2 convolution_bitcast_fusion
  462.7 87.9 %reduce-scatter.14.cloned.1.call-done = f32[64,4,128]{2,0,1:T(8,128)} async-done(((f32[2048,4,128]{2,0,1:T(8,128)}), f32[64,4,128]{2,0,1:T(8,128)}) %reduce-scatter.14.cloned.1.call-update) | async-done | bytes 131088 | tf_op jit(solution)/shard_map/reduce_scatter | solution.py:56
  552.3 37.3 %reduce-scatter.16.cloned.1.call-done = f32[64,1,128]{2,0,1:T(8,128)} async-done(((f32[64,8,128]{2,0,1:T(8,128)}), f32[64,1,128]{2,0,1:T(8,128)}) %reduce-scatter.16.cloned.1.call-update) | async-done | bytes 32784 | tf_op jit(solution)/shard_map/reduce_scatter | solution.py:73
  589.6 5.7 convolution_bitcast_fusion.3
  595.4 84.9 %reduce-scatter.18.cloned.1.call-done = f32[64,2,128]{2,0,1:T(8,128)} async-done(((f32[2048,2,128]{2,0,1:T(8,128)}), f32[64,2,128]{2,0,1:T(8,128)}) %reduce-scatter.18.cloned.1.call-update) | async-done | bytes 65552 | tf_op jit(solution)/shard_map/reduce_scatter | solution.py:56
  681.9 37.1 %reduce-scatter.20.cloned.1.call-done = f32[64,1,128]{2,0,1:T(8,128)} async-done(((f32[64,8,128]{2,0,1:T(8,128)}), f32[64,1,128]{2,0,1:T(8,128)}) %reduce-scatter.20.cloned.1.call-update) | async-done | bytes 32784 | tf_op jit(solution)/shard_map/reduce_scatter | solution.py:73
  719.1 5.7 convolution_bitcast_fusion.2
  724.9 84.9 %reduce-scatter.22.cloned.1.call-done = f32[64,2,128]{2,0,1:T(8,128)} async-done(((f32[2048,2,128]{2,0,1:T(8,128)}), f32[64,2,128]{2,0,1:T(8,128)}) %reduce-scatter.22.cloned.1.call-update) | async-done | bytes 65552 | tf_op jit(solution)/shard_map/reduce_scatter | solution.py:56
  811.5 37.5 %reduce-scatter.24.cloned.1.call-done = f32[64,1,128]{2,0,1:T(8,128)} async-done(((f32[64,8,128]{2,0,1:T(8,128)}), f32[64,1,128]{2,0,1:T(8,128)}) %reduce-scatter.24.cloned.1.call-update) | async-done | bytes 32784 | tf_op jit(solution)/shard_map/reduce_scatter | solution.py:73
  852.5 83.7 %reduce-scatter.26.cloned.1.call-done = f32[64,1,128]{2,0,1:T(8,128)} async-done(((f32[2048,1,128]{2,0,1:T(8,128)}), f32[64,1,128]{2,0,1:T(8,128)}) %reduce-scatter.26.cloned.1.call-update) | async-done | bytes 32784 | tf_op jit(solution)/shard_map/reduce_scatter | solution.py:56
  (144 shorter events, 68.7 us)
Async XLA Ops:
  8.5 22.1 %all-to-all-start = ((f32[32,1,64,128]{3,2,1,0:T(8,128)}), f32[32,1,64,128]{3,2,1,0:T(8,128)S(1)}, u32[]{:S(2)}, u32[]{:S(2)}) async-start(f32[32,1,64,128]{3,2,1,0:T(8,128)} %stack.60), calls=%async_computation | async-start | bytes 2097152 | tf_op jit(solution)/shard_map/all_to_all | solution.py:45
  31.3 6.1 collective-permute-start
  32.6 6.1 collective-permute-start.1
  40.9 33.1 %all-to-all-start.1 = ((f32[32,2,64,128]{3,2,1,0:T(8,128)}), f32[32,2,64,128]{3,2,1,0:T(8,128)}, u32[]{:S(2)}, u32[]{:S(2)}) async-start(f32[32,2,64,128]{3,2,1,0:T(8,128)} %stack.65), calls=%async_computation.1 | async-start | bytes 4194304 | tf_op jit(solution)/shard_map/all_to_all | solution.py:45
  77.8 6.2 collective-permute-start.2
  79.1 6.4 collective-permute-start.3
  87.8 33.8 %all-to-all-start.2 = ((f32[32,2,64,128]{3,2,1,0:T(8,128)}), f32[32,2,64,128]{3,2,1,0:T(8,128)}, u32[]{:S(2)}, u32[]{:S(2)}) async-start(f32[32,2,64,128]{3,2,1,0:T(8,128)} %stack.70), calls=%async_computation.2 | async-start | bytes 4194304 | tf_op jit(solution)/shard_map/all_to_all | solution.py:45
  125.3 17.2 %collective-permute-start.4 = (f32[64,128]{1,0:T(8,128)S(1)}, f32[64,128]{1,0:T(8,128)S(1)}, u32[]{:S(2)}, u32[]{:S(2)}) collective-permute-start(f32[64,128]{1,0:T(8,128)S(1)} %bitcast.125), channel_id=1, source_target_pairs={{96,0},{128,32},{160,64},{192,96},{224,128},{97,1},{129,33},{161,6... | collective-permute-start | bytes 98312 | tf_op jit(solution)/shard_map/ppermute | solution.py:12
  126.6 23.7 %collective-permute-start.5 = (f32[64,128]{1,0:T(8,128)S(1)}, f32[64,128]{1,0:T(8,128)S(1)}, u32[]{:S(2)}, u32[]{:S(2)}) collective-permute-start(f32[64,128]{1,0:T(8,128)S(1)} %bitcast.126), channel_id=1, source_target_pairs={{64,0},{96,32},{128,64},{160,96},{192,128},{224,160},{65,1},{97,33... | collective-permute-start | bytes 98312 | tf_op jit(solution)/shard_map/ppermute | solution.py:12
  127.9 22.5 %collective-permute-start.6 = (f32[64,128]{1,0:T(8,128)S(1)}, f32[64,128]{1,0:T(8,128)S(1)}, u32[]{:S(2)}, u32[]{:S(2)}) collective-permute-start(f32[64,128]{1,0:T(8,128)S(1)} %bitcast.127), channel_id=1, source_target_pairs={{32,0},{64,32},{96,64},{128,96},{160,128},{192,160},{224,192},{33,... | collective-permute-start | bytes 98312 | tf_op jit(solution)/shard_map/ppermute | solution.py:12
  129.2 21.2 %collective-permute-start.7 = (f32[64,128]{1,0:T(8,128)S(1)}, f32[64,128]{1,0:T(8,128)S(1)}, u32[]{:S(2)}, u32[]{:S(2)}) collective-permute-start(f32[64,128]{1,0:T(8,128)S(1)} %bitcast.128), channel_id=1, source_target_pairs={{0,32},{32,64},{64,96},{96,128},{128,160},{160,192},{192,224},{1,3... | collective-permute-start | bytes 98312 | tf_op jit(solution)/shard_map/ppermute | solution.py:12
  134.1 16.4 %collective-permute-start.8 = (f32[64,128]{1,0:T(8,128)S(1)}, f32[64,128]{1,0:T(8,128)S(1)}, u32[]{:S(2)}, u32[]{:S(2)}) collective-permute-start(f32[64,128]{1,0:T(8,128)S(1)} %bitcast.129), channel_id=1, source_target_pairs={{0,64},{32,96},{64,128},{96,160},{128,192},{160,224},{1,65},{33,97... | collective-permute-start | bytes 98312 | tf_op jit(solution)/shard_map/ppermute | solution.py:12
  142.6 9.4 collective-permute-start.9
  155.1 58.4 %all-to-all-start.3 = ((f32[32,4,64,128]{3,2,1,0:T(8,128)}), f32[32,4,64,128]{3,2,1,0:T(8,128)}, u32[]{:S(2)}, u32[]{:S(2)}) async-start(f32[32,4,64,128]{3,2,1,0:T(8,128)} %stack.79), calls=%async_computation.3 | async-start | bytes 8388608 | tf_op jit(solution)/shard_map/all_to_all | solution.py:45
  219.7 14.3 %collective-permute-start.10 = (f32[64,128]{1,0:T(8,128)S(1)}, f32[64,128]{1,0:T(8,128)S(1)}, u32[]{:S(2)}, u32[]{:S(2)}) collective-permute-start(f32[64,128]{1,0:T(8,128)S(1)} %fusion.10), channel_id=1, source_target_pairs={{96,0},{128,32},{160,64},{192,96},{224,128},{97,1},{129,33},{161,6... | collective-permute-start | bytes 98312 | tf_op jit(solution)/shard_map/ppermute | solution.py:12
  221.0 20.5 %collective-permute-start.11 = (f32[64,128]{1,0:T(8,128)S(1)}, f32[64,128]{1,0:T(8,128)S(1)}, u32[]{:S(2)}, u32[]{:S(2)}) collective-permute-start(f32[64,128]{1,0:T(8,128)S(1)} %fusion.10), channel_id=1, source_target_pairs={{64,0},{96,32},{128,64},{160,96},{192,128},{224,160},{65,1},{97,33... | collective-permute-start | bytes 98312 | tf_op jit(solution)/shard_map/ppermute | solution.py:12
  222.3 19.2 %collective-permute-start.12 = (f32[64,128]{1,0:T(8,128)S(1)}, f32[64,128]{1,0:T(8,128)S(1)}, u32[]{:S(2)}, u32[]{:S(2)}) collective-permute-start(f32[64,128]{1,0:T(8,128)S(1)} %fusion.10), channel_id=1, source_target_pairs={{32,0},{64,32},{96,64},{128,96},{160,128},{192,160},{224,192},{33,... | collective-permute-start | bytes 98312 | tf_op jit(solution)/shard_map/ppermute | solution.py:12
  223.6 18.0 %collective-permute-start.13 = (f32[64,128]{1,0:T(8,128)S(1)}, f32[64,128]{1,0:T(8,128)S(1)}, u32[]{:S(2)}, u32[]{:S(2)}) collective-permute-start(f32[64,128]{1,0:T(8,128)S(1)} %fusion.10), channel_id=1, source_target_pairs={{0,32},{32,64},{64,96},{96,128},{128,160},{160,192},{192,224},{1,3... | collective-permute-start | bytes 98312 | tf_op jit(solution)/shard_map/ppermute | solution.py:12
  228.2 13.4 %collective-permute-start.14 = (f32[64,128]{1,0:T(8,128)S(1)}, f32[64,128]{1,0:T(8,128)S(1)}, u32[]{:S(2)}, u32[]{:S(2)}) collective-permute-start(f32[64,128]{1,0:T(8,128)S(1)} %fusion.10), channel_id=1, source_target_pairs={{0,64},{32,96},{64,128},{96,160},{128,192},{160,224},{1,65},{33,97... | collective-permute-start | bytes 98312 | tf_op jit(solution)/shard_map/ppermute | solution.py:12
  234.0 9.1 collective-permute-start.15
  246.3 59.6 %all-to-all-start.4 = ((f32[32,4,64,128]{3,2,1,0:T(8,128)}), f32[32,4,64,128]{3,2,1,0:T(8,128)}, u32[]{:S(2)}, u32[]{:S(2)}) async-start(f32[32,4,64,128]{3,2,1,0:T(8,128)} %stack.88), calls=%async_computation.4 | async-start | bytes 8388608 | tf_op jit(solution)/shard_map/all_to_all | solution.py:45
  255.7 158.7 %reduce-scatter.10.cloned.1.call-start = ((), (), s32[]{:S(2)}) async-start(), calls=%async_computation.14 | async-start | bytes 4325376 | tf_op jit(solution)/shard_map/reduce_scatter | solution.py:56
  321.0 132.4 %reduce-scatter.12.cloned.1.call-start = ((), (), s32[]{:S(2)}) async-start(), calls=%async_computation.15 | async-start | bytes 294912 | tf_op jit(solution)/shard_map/reduce_scatter | solution.py:73
  416.0 134.6 %reduce-scatter.14.cloned.1.call-start = ((), (), s32[]{:S(2)}) async-start(), calls=%async_computation.16 | async-start | bytes 4325376 | tf_op jit(solution)/shard_map/reduce_scatter | solution.py:56
  462.6 127.0 %reduce-scatter.16.cloned.1.call-start = ((), (), s32[]{:S(2)}) async-start(), calls=%async_computation.17 | async-start | bytes 294912 | tf_op jit(solution)/shard_map/reduce_scatter | solution.py:73
  552.3 128.0 %reduce-scatter.18.cloned.1.call-start = ((), (), s32[]{:S(2)}) async-start(), calls=%async_computation.18 | async-start | bytes 2162688 | tf_op jit(solution)/shard_map/reduce_scatter | solution.py:56
  595.3 123.7 %reduce-scatter.20.cloned.1.call-start = ((), (), s32[]{:S(2)}) async-start(), calls=%async_computation.19 | async-start | bytes 294912 | tf_op jit(solution)/shard_map/reduce_scatter | solution.py:73
  681.9 127.9 %reduce-scatter.22.cloned.1.call-start = ((), (), s32[]{:S(2)}) async-start(), calls=%async_computation.20 | async-start | bytes 2162688 | tf_op jit(solution)/shard_map/reduce_scatter | solution.py:56
  724.8 211.4 %copy-start.13 = (f32[64,1,128]{2,0,1:T(8,128)S(1)}, f32[64,1,128]{2,0,1:T(8,128)}, u32[]{:S(2)}) copy-start(f32[64,1,128]{2,0,1:T(8,128)} %reduce-scatter.12.cloned.1.call-done) | copy-start | bytes 98308
  724.8 211.4 %copy-start.14 = (f32[64,1,128]{2,0,1:T(8,128)S(1)}, f32[64,1,128]{2,0,1:T(8,128)}, u32[]{:S(2)}) copy-start(f32[64,1,128]{2,0,1:T(8,128)} %reduce-scatter.20.cloned.1.call-done) | copy-start | bytes 98308
  724.8 124.1 %reduce-scatter.24.cloned.1.call-start = ((), (), s32[]{:S(2)}) async-start(), calls=%async_computation.21 | async-start | bytes 294912 | tf_op jit(solution)/shard_map/reduce_scatter | solution.py:73
  811.4 124.8 %reduce-scatter.26.cloned.1.call-start = ((), (), s32[]{:S(2)}) async-start(), calls=%async_computation.22 | async-start | bytes 1081344 | tf_op jit(solution)/shard_map/reduce_scatter | solution.py:56
  (16 other events, 375.1 us)
Sparse Core Ops, SparseCore 0:
  321.1 93.1 reduce-scatter.9
  417.0 36.3 reduce-scatter.11
  462.8 87.8 reduce-scatter.13
  553.1 36.4 reduce-scatter.15
  595.5 84.7 reduce-scatter.17
  682.7 36.3 reduce-scatter.19
  724.9 84.8 reduce-scatter.21
  812.5 36.3 reduce-scatter.23
  852.7 83.4 reduce-scatter.25
